TPU v7x, 32 devices: a whole 2x2x4 slice. The times are simulated.
32 devices in a mesh: gx: 4 (over x, core), gy: 2 (over y), gz: 4 (over z).
Axes of the slice: x: 2, y: 2, z: 4, core: 2. Of those that a mesh axis runs over, the one named last changes fastest.
Arguments:
- positions: float32 [3, 4, 2, 4, 32], P(None, 'gx', 'gy', 'gz'), as said below
- species: int32 [4, 2, 4, 32], P('gx', 'gy', 'gz'), may hold values from 0 to 88
- atom_count: int32 [4, 2, 4], P('gx', 'gy', 'gz'), may hold values from 16 to 32, as said below
- edge_count: int32 [4, 2, 4], P('gx', 'gy', 'gz'), may hold values from 0 to 1792, as said below
- sender: int32 [4, 2, 4, 1792], P('gx', 'gy', 'gz'), may hold values from 0 to 863, as said below
- receiver: int32 [4, 2, 4, 1792], P('gx', 'gy', 'gz'), may hold values from 0 to 31, as said below
- image_shift: int32 [3, 4, 2, 4, 1792], P(None, 'gx', 'gy', 'gz'), may hold values from -1 to 1, as said below
- embed: float32 [89, 128], replicated, may hold values from -6 to 6
- radial_in: float32 [2, 8, 64], replicated, may hold values from -2 to 2
- radial_out: float32 [2, 64, 384], replicated, may hold values from -0.75 to 0.75
- w_up: float32 [2, 128, 128], replicated, may hold values from -0.5 to 0.5
- lam: float32 [2, 2, 128], replicated, may hold values from -4 to 4
- w_mix: float32 [2, 128, 128], replicated, may hold values from -0.5 to 0.5
- read_one: float32 [128], replicated, may hold values from -0.5 to 0.5
- read_hidden: float32 [128, 16], replicated, may hold values from -0.5 to 0.5
- read_out: float32 [16], replicated, may hold values from -1.5 to 1.5
Outputs:
- site_energy: float32 [4, 2, 4, 32], P('gx', 'gy', 'gz')
- forces: float32 [3, 4, 2, 4, 32], P(None, 'gx', 'gy', 'gz')
Inputs may be any that keep to these rules, and one draw needn't show every extreme that they name: `atom_count`: slots at and above a brick's count are empty: no edge names them, and their species and positions are placeholders. At least one brick is full. `edge_count`: some brick has all 1792 edge slots live. A live edge names an owned slot of the neighbour block; sender and receiver are 0 on edges that are not live. Each live edge's image-shifted sender lies within 5.5 angstrom of its receiver; every pair of owned atoms within 5 angstrom of each other, over all periodic images, is a live edge of the receiver's brick; the (sender image, receiver) pairs within a brick are distinct. A live edge's receiver is below atom_count. `image_shift`: nonzero only where the neighbour block lies across the box's boundary; 0 on edges that are not live. `positions`: any two atoms are at least 1 angstrom apart.
All inputs are finite; a program needn't handle non-finite values.
Results may differ from a plain program's by a relative error of at most 0.0085.
Values may be sent and summed in bfloat16 or wider, within the bound.
A program may use at most 128 MiB of HBM per device.

v0:
```python
import functools
import itertools

import jax
import jax.numpy as jnp
from jax import lax
from jax.experimental import pallas as pl
from jax.experimental.pallas import tpu as pltpu
from jax.sharding import PartitionSpec as P

cutoff_radius = 5.0
lattice_step = 2.25
mean_degree = 8.0
F32 = jnp.float32
BF16 = jnp.bfloat16
MESH = pl.DeviceIdType.MESH
CH = 256


def dg(a, b, ca, cb):
    return lax.dot_general(a, b, (((ca,), (cb,)), ((), ())), preferred_element_type=F32)


def split(x):
    hi = x.astype(BF16)
    return hi, (x - hi.astype(F32)).astype(BF16)


def dg3(a, b, ca, cb):
    ah, al = split(a)
    bh, bl = split(b)
    return dg(ah, bh, ca, cb) + (dg(ah, bl, ca, cb) + dg(al, bh, ca, cb))


def parts(x):
    p1 = x.astype(BF16).astype(F32)
    p2 = (x - p1).astype(BF16).astype(F32)
    p3 = x - p1 - p2
    return jnp.concatenate([p1, p2, p3, jnp.zeros_like(x)], axis=0).astype(BF16)


def whole(y):
    return y[0:8] + y[8:16] + y[16:24]


def offsets_of(sizes):
    per_axis = [(-1, 0, 1) if n >= 3 else (-1, 0) if n == 2 else (0,) for n in sizes]
    return list(itertools.product(*per_axis))


def kernel(
    sizes,
    counts,
    pos_ref,
    spec_ref,
    sender_ref,
    receiver_ref,
    shift_ref,
    embed_ref,
    win_ref,
    wout_ref,
    wup_ref,
    lam_ref,
    wmix_ref,
    rone_ref,
    rhid_ref,
    rout_ref,
    energy_ref,
    force_ref,
    own8,
    gpos_in,
    h_own,
    h_in,
    dl_out,
    dl_in,
    dp_out,
    dp_in,
    emb_s,
    ohs,
    ohr,
    pool,
    rad,
    lift,
    base,
    pre_s,
    der,
    dlift,
    rows,
    drow,
    send_sem,
    recv_sem,
):
    atoms = pos_ref.shape[1]
    edges = sender_ref.shape[1]
    nb = win_ref.shape[1]
    rh = win_ref.shape[2]
    width = embed_ref.shape[1]
    nspec = embed_ref.shape[0]
    spad = emb_s.shape[0]
    offs = offsets_of(sizes)
    total = len(offs)
    tiles = dp_out.shape[0]
    ghosts = tiles * 128
    here = offs.index(tuple(0 for _ in sizes))
    me = [lax.axis_index(a) for a in ("gx", "gy", "gz")]

    def device(off, sign):
        return tuple(
            lax.rem(m + (sign * o) % n, n) if o else m for m, o, n in zip(me, off, sizes)
        )

    others = [u for u in range(total) if u != here]

    barrier = pltpu.get_barrier_semaphore()
    for u in others:
        pl.semaphore_signal(barrier, inc=1, device_id=device(offs[u], 1), device_id_type=MESH)

    own8[...] = jnp.zeros_like(own8)
    mine = jnp.concatenate([pos_ref[...], spec_ref[...].astype(F32)], axis=0)
    own8[0:4, :] = jnp.concatenate([mine] * 4, axis=1)
    pl.semaphore_wait(barrier, len(others))

    def copy(phase, u, src, dst, sign):
        return pltpu.make_async_remote_copy(
            src_ref=src,
            dst_ref=dst,
            send_sem=send_sem.at[phase, u],
            recv_sem=recv_sem.at[phase, u],
            device_id=device(offs[u], sign),
            device_id_type=MESH,
        )

    sent = []

    def exchange(phase, source, target, sign):
        started = [copy(phase, u, source(u), target.at[u], sign) for u in others]
        for c in started:
            c.start()
        sent.extend(started)
        return started

    first = exchange(0, lambda u: own8, gpos_in, -1)

    gpos_in[here] = own8[...]
    send_id = sender_ref[...]
    block = jnp.right_shift(send_id, 5)
    slot = send_id - block * 32
    bx = (block >= 9).astype(jnp.int32) + (block >= 18).astype(jnp.int32)
    rest = block - 9 * bx
    by = (rest >= 3).astype(jnp.int32) + (rest >= 6).astype(jnp.int32)
    bz = rest - 3 * by
    flat = jnp.zeros_like(block)
    for d, n in zip((bx, by, bz), sizes):
        if n >= 3:
            flat = flat * 3 + d
        elif n == 2:
            flat = flat * 2 + jnp.where(d == 1, 1, 0)
    ghost_id = flat * 32 + slot
    sub = lax.broadcasted_iota(jnp.int32, (128, CH), 0)
    for e in range(0, edges, CH):
        for t in range(tiles):
            ohs[t * 128 : (t + 1) * 128, e : e + CH] = jnp.where(
                sub == ghost_id[:, e : e + CH] - t * 128, 1.0, 0.0
            ).astype(BF16)
    recv_id = receiver_ref[...]
    near = lax.broadcasted_iota(jnp.int32, (atoms, edges), 0) == recv_id
    ohr[...] = jnp.where(near, 1.0, 0.0).astype(BF16)
    at_recv = whole(dg(parts(own8[...])[:, 0:atoms], ohr[...], 1, 0))
    emb_s[...] = jnp.zeros_like(emb_s)
    emb_s[0:nspec, :] = embed_ref[...]
    emb = emb_s[...].astype(BF16)
    wu_h, wu_l = split(wup_ref[0])
    table = (dg(emb, wu_h, 1, 0) + dg(emb, wu_l, 1, 0)).astype(BF16)
    kind = lax.broadcasted_iota(jnp.int32, (spad, 128), 0).astype(F32)
    own_kind = jnp.where(kind == own8[3:4, :], 1.0, 0.0).astype(BF16)
    h0 = dg(own_kind, emb, 0, 0)[0:atoms]
    valid = lax.broadcasted_iota(jnp.int32, (1, edges), 1) < counts[1]
    atom_row = (lax.broadcasted_iota(jnp.int32, (1, atoms), 1) < counts[0]).astype(F32)
    atom_col = (lax.broadcasted_iota(jnp.int32, (atoms, width), 0) < counts[0]).astype(F32)
    if h_in.shape[0] > total:
        h_in[total:] = jnp.zeros((h_in.shape[0] - total, atoms, width), BF16)
    dp_out[...] = jnp.zeros_like(dp_out)

    for c in first:
        c.wait_recv()

    lane = lax.broadcasted_iota(jnp.int32, (8, 128), 1)
    cols = []
    for t in range(tiles):
        tile = jnp.zeros((8, 128), F32)
        for j in range(4):
            if 4 * t + j < total:
                inside = (lane >= 32 * j) & (lane < 32 * j + 32)
                tile = jnp.where(inside, gpos_in[4 * t + j], tile)
        cols.append(tile)
    gpos = jnp.concatenate(cols, axis=1)
    gkind = jnp.concatenate(
        [jnp.where(kind == c[3:4, :], 1.0, 0.0).astype(BF16) for c in cols], axis=1
    )
    ghost_lift = dg(table, gkind, 0, 0).astype(BF16)
    lhs = jnp.concatenate([ghost_lift, parts(gpos)], axis=0)
    at_send = []
    for e in range(0, edges, CH):
        got = dg(lhs, ohs[:, e : e + CH], 1, 0)
        lift[0, :, e : e + CH] = got[0:width]
        at_send.append(whole(got[width:]))
    at_send = jnp.concatenate(at_send, axis=1)

    def axis(a, n, cells):
        length = n * cells * lattice_step
        moved = at_send[a : a + 1] + shift_ref[a : a + 1].astype(F32) * length
        return (moved - at_recv[a : a + 1]) / cutoff_radius

    x = axis(0, sizes[0], 4)
    y = axis(1, sizes[1], 4)
    z = axis(2, sizes[2], atoms // 16)
    dist2 = x * x + y * y + z * z
    inner = jnp.where(valid, jnp.maximum(1.0 - dist2, 0.0), 0.0)
    env = inner * inner
    s3, s5, s15 = 3.0**0.5, 5.0**0.5, 15.0**0.5
    harm = [
        jnp.ones_like(x),
        s3 * x,
        s3 * y,
        s3 * z,
        s15 * x * y,
        s15 * y * z,
        s15 * x * z,
        0.5 * s15 * (x * x - y * y),
        0.5 * s5 * (2.0 * z * z - x * x - y * y),
    ]
    rows[0:1] = x
    rows[1:2] = y
    rows[2:3] = z
    rows[3:4] = dist2
    rows[4:5] = inner
    for m in range(9):
        rows[8 + m : 9 + m] = harm[m] * (1.0 / mean_degree)
        weight = harm[m] * env * (1.0 / mean_degree)
        pool[atoms * m : atoms * (m + 1), :] = jnp.where(near, weight, 0.0).astype(BF16)

    centres = lax.broadcasted_iota(jnp.int32, (nb, edges), 0).astype(F32) / (nb - 1)

    def basis_of():
        return jnp.exp(-jnp.square((rows[3:4] - centres) * nb))

    def radial(t):
        basis = basis_of()
        bh = basis.astype(BF16).astype(F32)
        bl = basis - bh
        wi = win_ref[t]
        wh = wi.astype(BF16).astype(F32)
        wl = wi - wh
        pre = dg(
            jnp.concatenate([wh, wh, wl, wl], axis=0).astype(BF16),
            jnp.concatenate([bh, bl, bh, bl], axis=0).astype(BF16),
            0,
            0,
        )
        pre_s[t] = pre
        hidden = pre * jax.nn.sigmoid(pre)
        hh, hl = split(hidden)
        oh, ol = split(wout_ref[t])
        left = jnp.concatenate([oh, oh, ol], axis=0)
        right = jnp.concatenate([hh, hl, hh], axis=0)
        for e in range(0, edges, CH):
            rad[t, :, e : e + CH] = dg(left, right[:, e : e + CH], 0, 0)

    def pooled(t):
        for e in range(0, edges, CH):
            up = lift[t, :, e : e + CH]
            for k in range(3):
                base[t, k * width : (k + 1) * width, e : e + CH] = (
                    rad[t, k * width : (k + 1) * width, e : e + CH] * up
                ).astype(BF16)
        a0 = dg(pool[0:atoms], base[t, 0:width], 1, 1)
        a1 = dg(pool[atoms : 4 * atoms], base[t, width : 2 * width], 1, 1)
        a2 = dg(pool[4 * atoms : 9 * atoms], base[t, 2 * width : 3 * width], 1, 1)
        a1 = [a1[atoms * m : atoms * (m + 1)] for m in range(3)]
        a2 = [a2[atoms * m : atoms * (m + 1)] for m in range(5)]
        l0, l1 = lam_ref[t, 0:1], lam_ref[t, 1:2]
        q1 = sum(a * a for a in a1)
        q2 = sum(a * a for a in a2)
        return a0 + l0 * q1 + l1 * q2, a1, a2

    def pulled(t, d_prod, a1, a2):
        l0, l1 = lam_ref[t, 0:1], lam_ref[t, 1:2]
        g1 = 2.0 * l0 * d_prod
        g2 = 2.0 * l1 * d_prod
        d_a = [
            d_prod,
            jnp.concatenate([g1 * a for a in a1], axis=0),
            jnp.concatenate([g2 * a for a in a2], axis=0),
        ]
        d_t = [d.T.astype(BF16) for d in d_a]
        d_a = [d.astype(BF16) for d in d_a]
        span = [(0, 1), (1, 4), (4, 9)]
        for e in range(0, edges, CH):
            up = lift[t, :, e : e + CH]
            d_up = jnp.zeros((width, CH), F32)
            for k, (lo, hi) in enumerate(span):
                d_base = dg(d_t[k], pool[lo * atoms : hi * atoms, e : e + CH], 1, 0)
                d_up = d_up + d_base * rad[t, k * width : (k + 1) * width, e : e + CH]
                der[k * width : (k + 1) * width, e : e + CH] = (d_base * up).astype(BF16)
            if t == 1:
                dlift[:, e : e + CH] = d_up.astype(BF16)
        return d_a

    def edge_rows(t, d_a):
        span = [(0, 1), (1, 4), (4, 9)]
        for e in range(0, edges, CH):
            pick = ohr[:, e : e + CH].astype(F32)
            for k, (lo, hi) in enumerate(span):
                q = dg(d_a[k], base[t, k * width : (k + 1) * width, e : e + CH], 1, 0)
                for m in range(lo, hi):
                    part = q[(m - lo) * atoms : (m - lo + 1) * atoms] * pick
                    line = jnp.sum(part, axis=0, keepdims=True)
                    if t == 1:
                        drow[m : m + 1, e : e + CH] = line
                    else:
                        drow[m : m + 1, e : e + CH] += line
        d_hidden = dg(wout_ref[t].astype(BF16), der[...], 1, 0)
        pre = pre_s[t]
        sig = jax.nn.sigmoid(pre)
        d_pre = d_hidden * (sig * (1.0 + pre * (1.0 - sig)))
        d_basis = dg3(win_ref[t], d_pre, 1, 0)
        gap = rows[3:4] - centres
        slope = jnp.sum(d_basis * basis_of() * gap, axis=0, keepdims=True) * (-2.0 * nb * nb)
        if t == 1:
            drow[9:10] = slope
        else:
            drow[9:10] += slope

    radial(0)
    prod1, a1_one, a2_one = pooled(0)
    h1 = h0 + dg3(prod1, wmix_ref[0], 1, 0)
    h_own[...] = h1.astype(BF16)
    second = exchange(1, lambda u: h_own, h_in, -1)
    h_in[here] = h_own[...]
    rone = jnp.broadcast_to(rone_ref[...], (8, width))
    energy1 = dg3(rone, h1, 1, 1)[0:1]
    radial(1)
    wt_h, wt_l = split(wup_ref[1].T)
    for c in second:
        c.wait_recv()

    feats = h_in[...].reshape(ghosts, width)
    ghost_lift = (dg(wt_h, feats, 1, 1) + dg(wt_l, feats, 1, 1)).astype(BF16)
    for e in range(0, edges, CH):
        lift[1, :, e : e + CH] = dg(ghost_lift, ohs[:, e : e + CH], 1, 0)
    prod2, a1_two, a2_two = pooled(1)
    h2 = h_own[...].astype(F32) + dg3(prod2, wmix_ref[1], 1, 0)
    ro_pre = dg3(rhid_ref[...], h2, 1, 1)
    ro_sig = jax.nn.sigmoid(ro_pre)
    energy2 = jnp.sum(ro_pre * ro_sig * rout_ref[...], axis=0, keepdims=True)
    energy_ref[...] = (energy1 + energy2) * atom_row

    d_ro = rout_ref[...] * atom_row * (ro_sig * (1.0 + ro_pre * (1.0 - ro_sig)))
    d_h2 = dg3(d_ro, rhid_ref[...], 0, 0)
    d_prod2 = dg3(d_h2, wmix_ref[1], 1, 1)
    d_a = pulled(1, d_prod2, a1_two, a2_two)
    for t in range(tiles):
        d_ghost = dg(ohs[t * 128 : (t + 1) * 128], dlift[...], 1, 1)
        for j in range(4):
            if 4 * t + j < total:
                dl_out[4 * t + j] = d_ghost[32 * j : 32 * j + 32].astype(BF16)
    third = exchange(2, lambda u: dl_out.at[u], dl_in, 1)
    dl_in[here] = dl_out[here]
    edge_rows(1, d_a)
    for c in third:
        c.wait_recv()

    gathered = dl_in[0].astype(F32)
    for u in range(1, total):
        gathered = gathered + dl_in[u].astype(F32)
    d_h1 = d_h2 + dg3(gathered, wup_ref[1], 1, 1) + atom_col * rone_ref[...]
    d_prod1 = dg3(d_h1, wmix_ref[0], 1, 1)
    d_a = pulled(0, d_prod1, a1_one, a2_one)
    edge_rows(0, d_a)

    x, y, z, inner = rows[0:1], rows[1:2], rows[2:3], rows[4:5]
    env8 = inner * inner * (1.0 / mean_degree)
    d_env = drow[0:1] * rows[8:9]
    for m in range(1, 9):
        d_env = d_env + drow[m : m + 1] * rows[8 + m : 9 + m]
    d_dist = 2.0 * (drow[9:10] - 2.0 * d_env * inner)
    dh = [drow[m : m + 1] * env8 for m in range(9)]
    d_x = d_dist * x + s3 * dh[1] + s15 * (y * dh[4] + z * dh[6] + x * dh[7]) - s5 * x * dh[8]
    d_y = d_dist * y + s3 * dh[2] + s15 * (x * dh[4] + z * dh[5] - y * dh[7]) - s5 * y * dh[8]
    d_z = d_dist * z + s3 * dh[3] + s15 * (y * dh[5] + x * dh[6]) + 2.0 * s5 * z * dh[8]
    drow[0:1] = d_x / cutoff_radius
    drow[1:2] = d_y / cutoff_radius
    drow[2:3] = d_z / cutoff_radius
    drow[3:8] = jnp.zeros((5, edges), F32)
    d_rel = drow[0:8]
    d_hi = d_rel.astype(BF16).astype(F32)
    both = jnp.concatenate([d_hi, d_rel - d_hi], axis=0).astype(BF16)
    for t in range(tiles):
        back = dg(both, ohs[t * 128 : (t + 1) * 128], 1, 1)
        dp_out[t] = back[0:8] + back[8:16]
    fourth = exchange(3, lambda u: dp_out.at[u // 4], dp_in, 1)
    dp_in[here] = dp_out[here // 4]
    own = dg(both, ohr[...], 1, 1)
    for c in fourth:
        c.wait_recv()
    fold = jnp.zeros((8, 128), F32)
    for u in range(total):
        j = u % 4
        inside = (lane >= 32 * j) & (lane < 32 * j + 32)
        fold = fold + jnp.where(inside, dp_in[u], 0.0)
    fold = fold + pltpu.roll(fold, 64, 1)
    fold = fold + pltpu.roll(fold, 32, 1)
    force = own[0:8] + own[8:16] - fold[:, 0:atoms]
    force_ref[...] = force[0:3]
    for c in sent:
        c.wait_send()


def local(
    sizes,
    positions,
    species,
    atom_count,
    edge_count,
    sender,
    receiver,
    image_shift,
    embed,
    radial_in,
    radial_out,
    w_up,
    lam,
    w_mix,
    read_one,
    read_hidden,
    read_out,
):
    atoms = positions.shape[-1]
    edges = sender.shape[-1]
    nspec, width = embed.shape
    rh = radial_in.shape[2]
    total = len(offsets_of(sizes))
    tiles = (total + 3) // 4
    ghosts = tiles * 128
    counts = jnp.concatenate([atom_count.reshape(1), edge_count.reshape(1)])
    vmem = pl.BlockSpec(memory_space=pltpu.VMEM)
    energy, force = pl.pallas_call(
        functools.partial(kernel, sizes),
        out_shape=(
            jax.ShapeDtypeStruct((1, atoms), F32),
            jax.ShapeDtypeStruct((3, atoms), F32),
        ),
        in_specs=[pl.BlockSpec(memory_space=pltpu.SMEM)] + [vmem] * 14,
        out_specs=(vmem, vmem),
        scratch_shapes=[
            pltpu.VMEM((8, 128), F32),
            pltpu.VMEM((total, 8, 128), F32),
            pltpu.VMEM((atoms, width), BF16),
            pltpu.VMEM((4 * tiles, atoms, width), BF16),
            pltpu.VMEM((total, atoms, width), BF16),
            pltpu.VMEM((total, atoms, width), BF16),
            pltpu.VMEM((tiles, 8, 128), F32),
            pltpu.VMEM((total, 8, 128), F32),
            pltpu.VMEM(((nspec + 15) // 16 * 16, width), F32),
            pltpu.VMEM((ghosts, edges), BF16),
            pltpu.VMEM((atoms, edges), BF16),
            pltpu.VMEM((9 * atoms, edges), BF16),
            pltpu.VMEM((2, 3 * width, edges), F32),
            pltpu.VMEM((2, width, edges), F32),
            pltpu.VMEM((2, 3 * width, edges), BF16),
            pltpu.VMEM((2, rh, edges), F32),
            pltpu.VMEM((3 * width, edges), BF16),
            pltpu.VMEM((width, edges), BF16),
            pltpu.VMEM((24, edges), F32),
            pltpu.VMEM((16, edges), F32),
            pltpu.SemaphoreType.DMA((4, total)),
            pltpu.SemaphoreType.DMA((4, total)),
        ],
        compiler_params=pltpu.CompilerParams(
            collective_id=0, has_side_effects=True, vmem_limit_bytes=50 * 1024 * 1024
        ),
    )(
        counts,
        positions.reshape(3, atoms),
        species.reshape(1, atoms),
        sender.reshape(1, edges),
        receiver.reshape(1, edges),
        image_shift.reshape(3, edges),
        embed,
        radial_in,
        radial_out,
        w_up,
        lam,
        w_mix,
        read_one.reshape(1, width),
        read_hidden.T,
        read_out.reshape(-1, 1),
    )
    return energy.reshape(1, 1, 1, atoms), force.reshape(3, 1, 1, 1, atoms)


def solution(mesh):
    sizes = tuple(mesh.shape[a] for a in ("gx", "gy", "gz"))
    in_specs = (
        P(None, "gx", "gy", "gz", None),
        P("gx", "gy", "gz", None),
        P("gx", "gy", "gz"),
        P("gx", "gy", "gz"),
        P("gx", "gy", "gz", None),
        P("gx", "gy", "gz", None),
        P(None, "gx", "gy", "gz", None),
        P(),
        P(),
        P(),
        P(),
        P(),
        P(),
        P(),
        P(),
        P(),
    )
    out_specs = (P("gx", "gy", "gz", None), P(None, "gx", "gy", "gz", None))
    return jax.shard_map(
        functools.partial(local, sizes),
        mesh=mesh,
        in_specs=in_specs,
        out_specs=out_specs,
        check_vma=False,
    )
```

profile of v0, /device:TPU:0, one launch (start us, length us, event | category | flops | bytes accessed | tf_op | source)
XLA Modules:
  0.0 44.4 jit_solution(14318868009558227798)
XLA Ops:
  0.6 0.0 copy-start.3
  1.9 0.1 pad_add_fusion.counts
  2.0 0.7 %copy.25 = f32[3,1,1,1,32]{4,0,2,1,3:T(4,128)S(1)} copy(f32[3,1,1,1,32]{4,3,2,1,0:T(1,128)} %param.16) | data formatting | bytes 768
  2.7 0.7 %copy.18.rout_ref = f32[16,1]{1,0:T(8,128)S(1)} copy(f32[16,1]{0,1:T(1,128)} %bitcast.27) | data formatting | bytes 128 | tf_op jit(solution)/shard_map/reshape | solution.py:497
  3.4 0.0 copy-start.4
  3.4 0.0 copy-start.5
  3.4 0.0 copy-start.6
  3.4 0.0 copy-start.8
  3.5 0.8 %copy.24 = s32[3,1,1,1,1792]{4,0,2,1,3:T(4,128)S(1)} copy(s32[3,1,1,1,1792]{4,3,2,1,0:T(1,128)} %param.22) | data formatting | bytes 43008
  4.3 0.0 copy-start.10
  4.3 0.0 copy-done.3
  4.3 0.0 copy-done.4
  4.3 0.0 copy-done.5
  4.3 0.0 copy-done.6
  4.3 0.0 copy-done.7
  4.3 0.0 copy-done.8
  4.3 0.6 %copy-done.9 = s32[1,1,1,32]{3,2,1,0:T(1,128)S(1)} copy-done((s32[1,1,1,32]{3,2,1,0:T(1,128)S(1)}, s32[1,1,1,32]{3,2,1,0:T(1,128)}, u32[]{:S(2)}) %copy-start.9) | copy-done | bytes 152
  4.9 0.0 copy-done.10
  4.9 0.9 %copy-done = f32[2,64,384]{2,1,0:T(8,128)S(1)} copy-done((f32[2,64,384]{2,1,0:T(8,128)S(1)}, f32[2,64,384]{2,1,0:T(8,128)}, u32[]{:S(2)}) %copy-start) | copy-done | bytes 196632
  5.8 0.9 %copy-done.1 = f32[2,128,128]{2,1,0:T(8,128)S(1)} copy-done((f32[2,128,128]{2,1,0:T(8,128)S(1)}, f32[2,128,128]{2,1,0:T(8,128)}, u32[]{:S(2)}) %copy-start.1) | copy-done | bytes 131096
  6.7 0.9 %copy-done.2 = f32[2,128,128]{2,1,0:T(8,128)S(1)} copy-done((f32[2,128,128]{2,1,0:T(8,128)S(1)}, f32[2,128,128]{2,1,0:T(8,128)}, u32[]{:S(2)}) %copy-start.2) | copy-done | bytes 131096
  7.7 35.7 %shard_map.167 = (f32[1,32]{1,0:T(1,128)S(1)}, f32[3,32]{1,0:T(4,128)S(1)}) custom-call(s32[2]{0:T(128)S(1)} %pad_add_fusion.counts, f32[3,32]{1,0:T(4,128)S(1)} %bitcast.20, s32[1,32]{1,0:T(1,128)S(1)} %bitcast.24, s32[1,1792]{1,0:T(1,128)S(1)} %bitcast.21, s32[1,1792]{1,0:T(1,128)S(1)} %bitcast.22, s32[3,1792]{1,0:T(4,128)S(1)} %bitcast.18, ...), custom_call_target="tpu_custom_call" | custom-call | tf_op jit(solution)/shard_map/pallas_call | solution.py:447
  43.4 0.6 %copy.19 = f32[3,1,1,1,32]{4,3,2,1,0:T(1,128)} copy(f32[3,1,1,1,32]{4,0,3,2,1:T(4,128)S(1)} %bitcast.23) | data formatting | bytes 768
  43.9 0.5 %copy.29 = f32[1,1,1,32]{3,2,1,0:T(1,128)} copy(f32[1,1,1,32]{3,2,1,0:T(1,128)S(1)} %bitcast.26) | data formatting | bytes 256
  (5 shorter events, 0.0 us)
Async XLA Ops:
  0.6 3.6 %copy-start.3 = (f32[89,128]{1,0:T(8,128)S(1)}, f32[89,128]{1,0:T(8,128)}, u32[]{:S(2)}) copy-start(f32[89,128]{1,0:T(8,128)} %embed_ref.1) | copy-start | bytes 136708
  3.4 0.8 %copy-start.4 = (f32[2,8,64]{2,1,0:T(8,128)S(1)}, f32[2,8,64]{2,1,0:T(8,128)}, u32[]{:S(2)}) copy-start(f32[2,8,64]{2,1,0:T(8,128)} %win_ref.1) | copy-start | bytes 12292
  3.4 0.9 %copy-start.5 = (f32[128,16]{0,1:T(8,128)S(1)}, f32[128,16]{0,1:T(8,128)}, u32[]{:S(2)}) copy-start(f32[128,16]{0,1:T(8,128)} %param.30) | copy-start | bytes 24580
  3.4 0.9 %copy-start.6 = (s32[1,1,1,1792]{3,2,1,0:T(1,128)S(1)}, s32[1,1,1,1792]{3,2,1,0:T(1,128)}, u32[]{:S(2)}) copy-start(s32[1,1,1,1792]{3,2,1,0:T(1,128)} %param.20) | copy-start | bytes 21508
  3.4 0.9 %copy-start.7 = (s32[1,1,1,1792]{3,2,1,0:T(1,128)S(1)}, s32[1,1,1,1792]{3,2,1,0:T(1,128)}, u32[]{:S(2)}) copy-start(s32[1,1,1,1792]{3,2,1,0:T(1,128)} %param.21) | copy-start | bytes 21508
  3.4 0.9 %copy-start.8 = (f32[2,2,128]{2,1,0:T(2,128)S(1)}, f32[2,2,128]{2,1,0:T(2,128)}, u32[]{:S(2)}) copy-start(f32[2,2,128]{2,1,0:T(2,128)} %lam_ref.1) | copy-start | bytes 6148
  4.2 0.7 %copy-start.9 = (s32[1,1,1,32]{3,2,1,0:T(1,128)S(1)}, s32[1,1,1,32]{3,2,1,0:T(1,128)}, u32[]{:S(2)}) copy-start(s32[1,1,1,32]{3,2,1,0:T(1,128)} %param.17) | copy-start | bytes 388
  4.3 0.7 %copy-start.10 = (f32[128]{0:T(128)S(1)}, f32[128]{0:T(128)}, u32[]{:S(2)}) copy-start(f32[128]{0:T(128)} %param.29) | copy-start | bytes 1540
  4.9 0.9 %copy-start = (f32[2,64,384]{2,1,0:T(8,128)S(1)}, f32[2,64,384]{2,1,0:T(8,128)}, u32[]{:S(2)}) copy-start(f32[2,64,384]{2,1,0:T(8,128)} %wout_ref.1) | copy-start | bytes 589828
  5.8 0.9 %copy-start.1 = (f32[2,128,128]{2,1,0:T(8,128)S(1)}, f32[2,128,128]{2,1,0:T(8,128)}, u32[]{:S(2)}) copy-start(f32[2,128,128]{2,1,0:T(8,128)} %wup_ref.1) | copy-start | bytes 393220
  6.7 0.9 %copy-start.2 = (f32[2,128,128]{2,1,0:T(8,128)S(1)}, f32[2,128,128]{2,1,0:T(8,128)}, u32[]{:S(2)}) copy-start(f32[2,128,128]{2,1,0:T(8,128)} %wmix_ref.1) | copy-start | bytes 393220
where the time goes:
time: 44.8 us; the launch traced here: 44.4 us
  Pallas kernels  35.7 us (80%)
  local copies, waits for them, and re-layouts  6.63 us (15%)
  between operations  2.03 us (5%)
    pallas_call x1, Pallas kernels, local(): pl.pallas_call(functools.partial(kernel, sizes), out_shape=(jax.ShapeDtyp...  35.7 us
    unnamed x26, local copies, waits for them, and re-layouts  5.9 us

commit v1 on v0

--- a/solution.py
+++ b/solution.py
@@ -15,6 +15,7 @@
 BF16 = jnp.bfloat16
 MESH = pl.DeviceIdType.MESH
 CH = 256
+INPUTS = 16
 
 
 def dg(a, b, ca, cb):
@@ -50,23 +51,20 @@
 
 def kernel(
     sizes,
-    counts,
-    pos_ref,
-    spec_ref,
-    sender_ref,
-    receiver_ref,
-    shift_ref,
-    embed_ref,
-    win_ref,
-    wout_ref,
-    wup_ref,
-    lam_ref,
-    wmix_ref,
-    rone_ref,
-    rhid_ref,
-    rout_ref,
+    *refs,
+):
+    hbm = refs[:INPUTS]
+    energy_ref, force_ref = refs[INPUTS : INPUTS + 2]
+    held = refs[INPUTS + 2 : 2 * INPUTS + 2]
+    body(sizes, hbm, energy_ref, force_ref, held, *refs[2 * INPUTS + 2 :])
+
+
+def body(
+    sizes,
+    hbm,
     energy_ref,
     force_ref,
+    held,
     own8,
     gpos_in,
     h_own,
@@ -87,11 +85,36 @@
     dlift,
     rows,
     drow,
+    in_sem,
     send_sem,
     recv_sem,
 ):
-    atoms = pos_ref.shape[1]
-    edges = sender_ref.shape[1]
+    (
+        pos_ref,
+        spec_ref,
+        acount_ref,
+        ecount_ref,
+        sender_ref,
+        receiver_ref,
+        shift_ref,
+        embed_ref,
+        win_ref,
+        wout_ref,
+        wup_ref,
+        lam_ref,
+        wmix_ref,
+        rone_ref,
+        rhid_ref,
+        rout_ref,
+    ) = held
+    fetch = [
+        pltpu.make_async_copy(src, dst, in_sem.at[i])
+        for i, (src, dst) in enumerate(zip(hbm, held))
+    ]
+    for c in fetch:
+        c.start()
+    atoms = pos_ref.shape[-1]
+    edges = sender_ref.shape[-1]
     nb = win_ref.shape[1]
     rh = win_ref.shape[2]
     width = embed_ref.shape[1]
@@ -116,7 +139,11 @@
         pl.semaphore_signal(barrier, inc=1, device_id=device(offs[u], 1), device_id_type=MESH)
 
     own8[...] = jnp.zeros_like(own8)
-    mine = jnp.concatenate([pos_ref[...], spec_ref[...].astype(F32)], axis=0)
+    fetch[0].wait()
+    fetch[1].wait()
+    mine = jnp.concatenate(
+        [pos_ref[a, 0, 0] for a in range(3)] + [spec_ref[0, 0].astype(F32)], axis=0
+    )
     own8[0:4, :] = jnp.concatenate([mine] * 4, axis=1)
     pl.semaphore_wait(barrier, len(others))
 
@@ -132,8 +159,12 @@
 
     sent = []
 
-    def exchange(phase, source, target, sign):
-        started = [copy(phase, u, source(u), target.at[u], sign) for u in others]
+    def exchange(phase, source, target, sign, tile=None):
+        started = [
+            copy(phase, u, source(u), target.at[u], sign)
+            for u in others
+            if tile is None or u // 4 == tile
+        ]
         for c in started:
             c.start()
         sent.extend(started)
@@ -142,7 +173,9 @@
     first = exchange(0, lambda u: own8, gpos_in, -1)
 
     gpos_in[here] = own8[...]
-    send_id = sender_ref[...]
+    for c in fetch[2:]:
+        c.wait()
+    send_id = sender_ref[0, 0]
     block = jnp.right_shift(send_id, 5)
     slot = send_id - block * 32
     bx = (block >= 9).astype(jnp.int32) + (block >= 18).astype(jnp.int32)
@@ -162,7 +195,7 @@
             ohs[t * 128 : (t + 1) * 128, e : e + CH] = jnp.where(
                 sub == ghost_id[:, e : e + CH] - t * 128, 1.0, 0.0
             ).astype(BF16)
-    recv_id = receiver_ref[...]
+    recv_id = receiver_ref[0, 0]
     near = lax.broadcasted_iota(jnp.int32, (atoms, edges), 0) == recv_id
     ohr[...] = jnp.where(near, 1.0, 0.0).astype(BF16)
     at_recv = whole(dg(parts(own8[...])[:, 0:atoms], ohr[...], 1, 0))
@@ -174,12 +207,11 @@
     kind = lax.broadcasted_iota(jnp.int32, (spad, 128), 0).astype(F32)
     own_kind = jnp.where(kind == own8[3:4, :], 1.0, 0.0).astype(BF16)
     h0 = dg(own_kind, emb, 0, 0)[0:atoms]
-    valid = lax.broadcasted_iota(jnp.int32, (1, edges), 1) < counts[1]
-    atom_row = (lax.broadcasted_iota(jnp.int32, (1, atoms), 1) < counts[0]).astype(F32)
-    atom_col = (lax.broadcasted_iota(jnp.int32, (atoms, width), 0) < counts[0]).astype(F32)
+    valid = lax.broadcasted_iota(jnp.int32, (1, edges), 1) < ecount_ref[0]
+    atom_row = (lax.broadcasted_iota(jnp.int32, (1, atoms), 1) < acount_ref[0]).astype(F32)
+    atom_col = (lax.broadcasted_iota(jnp.int32, (atoms, width), 0) < acount_ref[0]).astype(F32)
     if h_in.shape[0] > total:
         h_in[total:] = jnp.zeros((h_in.shape[0] - total, atoms, width), BF16)
-    dp_out[...] = jnp.zeros_like(dp_out)
 
     for c in first:
         c.wait_recv()
@@ -208,7 +240,7 @@
 
     def axis(a, n, cells):
         length = n * cells * lattice_step
-        moved = at_send[a : a + 1] + shift_ref[a : a + 1].astype(F32) * length
+        moved = at_send[a : a + 1] + shift_ref[a, 0, 0].astype(F32) * length
         return (moved - at_recv[a : a + 1]) / cutoff_radius
 
     x = axis(0, sizes[0], 4)
@@ -260,11 +292,12 @@
         pre_s[t] = pre
         hidden = pre * jax.nn.sigmoid(pre)
         hh, hl = split(hidden)
-        oh, ol = split(wout_ref[t])
-        left = jnp.concatenate([oh, oh, ol], axis=0)
+        wo = wout_ref[t]
+        oh = wo.astype(BF16).astype(F32)
+        left = jnp.concatenate([oh, oh, wo - oh], axis=0).T.astype(BF16)
         right = jnp.concatenate([hh, hl, hh], axis=0)
         for e in range(0, edges, CH):
-            rad[t, :, e : e + CH] = dg(left, right[:, e : e + CH], 0, 0)
+            rad[t, :, e : e + CH] = dg(left, right[:, e : e + CH], 1, 0)
 
     def pooled(t):
         for e in range(0, edges, CH):
@@ -319,7 +352,8 @@
                         drow[m : m + 1, e : e + CH] = line
                     else:
                         drow[m : m + 1, e : e + CH] += line
-        d_hidden = dg(wout_ref[t].astype(BF16), der[...], 1, 0)
+        d_hidden = dg(jnp.concatenate(split(wout_ref[t]), axis=0), der[...], 1, 0)
+        d_hidden = d_hidden[0:rh] + d_hidden[rh : 2 * rh]
         pre = pre_s[t]
         sig = jax.nn.sigmoid(pre)
         d_pre = d_hidden * (sig * (1.0 + pre * (1.0 - sig)))
@@ -351,20 +385,25 @@
     prod2, a1_two, a2_two = pooled(1)
     h2 = h_own[...].astype(F32) + dg3(prod2, wmix_ref[1], 1, 0)
     ro_pre = dg3(rhid_ref[...], h2, 1, 1)
+    eye = lax.broadcasted_iota(jnp.int32, (ro_pre.shape[0],) * 2, 0) == (
+        lax.broadcasted_iota(jnp.int32, (ro_pre.shape[0],) * 2, 1)
+    )
+    rout = jnp.sum(jnp.where(eye, rout_ref[...], 0.0), axis=1, keepdims=True)
     ro_sig = jax.nn.sigmoid(ro_pre)
-    energy2 = jnp.sum(ro_pre * ro_sig * rout_ref[...], axis=0, keepdims=True)
-    energy_ref[...] = (energy1 + energy2) * atom_row
-
-    d_ro = rout_ref[...] * atom_row * (ro_sig * (1.0 + ro_pre * (1.0 - ro_sig)))
+    energy2 = jnp.sum(ro_pre * ro_sig * rout, axis=0, keepdims=True)
+    energy_ref[0, 0] = (energy1 + energy2) * atom_row
+
+    d_ro = rout * atom_row * (ro_sig * (1.0 + ro_pre * (1.0 - ro_sig)))
     d_h2 = dg3(d_ro, rhid_ref[...], 0, 0)
     d_prod2 = dg3(d_h2, wmix_ref[1], 1, 1)
     d_a = pulled(1, d_prod2, a1_two, a2_two)
+    third = []
     for t in range(tiles):
         d_ghost = dg(ohs[t * 128 : (t + 1) * 128], dlift[...], 1, 1)
         for j in range(4):
             if 4 * t + j < total:
                 dl_out[4 * t + j] = d_ghost[32 * j : 32 * j + 32].astype(BF16)
-    third = exchange(2, lambda u: dl_out.at[u], dl_in, 1)
+        third += exchange(2, lambda u: dl_out.at[u], dl_in, 1, t)
     dl_in[here] = dl_out[here]
     edge_rows(1, d_a)
     for c in third:
@@ -395,10 +434,11 @@
     d_rel = drow[0:8]
     d_hi = d_rel.astype(BF16).astype(F32)
     both = jnp.concatenate([d_hi, d_rel - d_hi], axis=0).astype(BF16)
+    fourth = []
     for t in range(tiles):
         back = dg(both, ohs[t * 128 : (t + 1) * 128], 1, 1)
         dp_out[t] = back[0:8] + back[8:16]
-    fourth = exchange(3, lambda u: dp_out.at[u // 4], dp_in, 1)
+        fourth += exchange(3, lambda u: dp_out.at[u // 4], dp_in, 1, t)
     dp_in[here] = dp_out[here // 4]
     own = dg(both, ohr[...], 1, 1)
     for c in fourth:
@@ -411,7 +451,8 @@
     fold = fold + pltpu.roll(fold, 64, 1)
     fold = fold + pltpu.roll(fold, 32, 1)
     force = own[0:8] + own[8:16] - fold[:, 0:atoms]
-    force_ref[...] = force[0:3]
+    for a in range(3):
+        force_ref[a, 0, 0] = force[a : a + 1]
     for c in sent:
         c.wait_send()
 
@@ -442,17 +483,35 @@
     total = len(offsets_of(sizes))
     tiles = (total + 3) // 4
     ghosts = tiles * 128
-    counts = jnp.concatenate([atom_count.reshape(1), edge_count.reshape(1)])
+    operands = (
+        positions,
+        species,
+        atom_count,
+        edge_count,
+        sender,
+        receiver,
+        image_shift,
+        embed,
+        radial_in,
+        radial_out,
+        w_up,
+        lam,
+        w_mix,
+        read_one.reshape(1, width),
+        read_hidden.T,
+        read_out.reshape(1, -1),
+    )
     vmem = pl.BlockSpec(memory_space=pltpu.VMEM)
     energy, force = pl.pallas_call(
         functools.partial(kernel, sizes),
         out_shape=(
-            jax.ShapeDtypeStruct((1, atoms), F32),
-            jax.ShapeDtypeStruct((3, atoms), F32),
+            jax.ShapeDtypeStruct((1, 1, 1, atoms), F32),
+            jax.ShapeDtypeStruct((3, 1, 1, 1, atoms), F32),
         ),
-        in_specs=[pl.BlockSpec(memory_space=pltpu.SMEM)] + [vmem] * 14,
+        in_specs=[pl.BlockSpec(memory_space=pltpu.HBM)] * INPUTS,
         out_specs=(vmem, vmem),
-        scratch_shapes=[
+        scratch_shapes=[pltpu.VMEM(a.shape, a.dtype) for a in operands]
+        + [
             pltpu.VMEM((8, 128), F32),
             pltpu.VMEM((total, 8, 128), F32),
             pltpu.VMEM((atoms, width), BF16),
@@ -473,30 +532,15 @@
             pltpu.VMEM((width, edges), BF16),
             pltpu.VMEM((24, edges), F32),
             pltpu.VMEM((16, edges), F32),
+            pltpu.SemaphoreType.DMA((INPUTS,)),
             pltpu.SemaphoreType.DMA((4, total)),
             pltpu.SemaphoreType.DMA((4, total)),
         ],
         compiler_params=pltpu.CompilerParams(
-            collective_id=0, has_side_effects=True, vmem_limit_bytes=50 * 1024 * 1024
+            collective_id=0, has_side_effects=True, vmem_limit_bytes=64 * 1024 * 1024
         ),
-    )(
-        counts,
-        positions.reshape(3, atoms),
-        species.reshape(1, atoms),
-        sender.reshape(1, edges),
-        receiver.reshape(1, edges),
-        image_shift.reshape(3, edges),
-        embed,
-        radial_in,
-        radial_out,
-        w_up,
-        lam,
-        w_mix,
-        read_one.reshape(1, width),
-        read_hidden.T,
-        read_out.reshape(-1, 1),
-    )
-    return energy.reshape(1, 1, 1, atoms), force.reshape(3, 1, 1, 1, atoms)
+    )(*operands)
+    return energy, force
 
 
 def solution(mesh):

time: 44.8 us -> 38.9 us (0.87)
  local copies, waits for them, and re-layouts: 6.63 us -> 1.69 us
  Pallas kernels: 35.7 us -> 35 us
    unnamed x26 -> x6, local copies, waits for them, and re-layouts: 5.9 us -> 1.69 us
    reshape x1 -> x0, local copies, waits for them, and re-layouts: 0.73 us -> none  [local(): read_out.reshape(-1, 1)]
    pallas_call x1, Pallas kernels: 35.7 us -> 35 us  [local(): pl.pallas_call(functools.partial(kernel, sizes), out_shape=(jax.ShapeDtyp...]
where the time goes in v1:
time: 38.9 us; the launch traced here: 38.7 us
  Pallas kernels  35 us (90%)
  between operations  1.95 us (5%)
  local copies, waits for them, and re-layouts  1.69 us (4%)
    pallas_call x1, Pallas kernels, local(): pl.pallas_call(functools.partial(kernel, sizes), out_shape=(jax.ShapeDtyp...  35 us
    unnamed x6, local copies, waits for them, and re-layouts  1.69 us

profile of v1, /device:TPU:0, one launch (start us, length us, event | category | flops | bytes accessed | tf_op | source)
XLA Modules:
  0.0 38.7 jit_solution(3105734492384455846)
XLA Ops:
  1.9 35.0 %shard_map.167 = (f32[1,1,1,32]{3,2,1,0:T(1,128)}, f32[3,1,1,1,32]{4,3,2,1,0:T(1,128)}) custom-call(f32[3,1,1,1,32]{4,3,2,1,0:T(1,128)} %refs_0_.1, s32[1,1,1,32]{3,2,1,0:T(1,128)} %refs_1_.1, s32[1,1,1]{2,1,0:T(1,128)S(6)} %copy.20.refs_2_, s32[1,1,1]{2,1,0:T(1,128)S(6)} %copy.21.refs_3_, s32[1,1,1,1792]{3,2,1,0:T(1,128)} %refs_4_.1, ...), custom_call_target="tpu_custom_call" | custom-call | tf_op jit(solution)/shard_map/pallas_call | solution.py:505
  37.0 0.0 copy-start.1
  37.0 0.0 copy-start
  37.0 0.6 %copy-done.1 = f32[1,1,1,32]{3,2,1,0:T(1,128)S(1)} copy-done((f32[1,1,1,32]{3,2,1,0:T(1,128)S(1)}, f32[1,1,1,32]{3,2,1,0:T(1,128)}, u32[]{:S(2)}) %copy-start.1) | copy-done | bytes 152
  37.6 0.5 %copy.22 = f32[1,1,1,32]{3,2,1,0:T(1,128)} copy(f32[1,1,1,32]{3,2,1,0:T(1,128)S(1)} %copy-done.1) | data formatting | bytes 256
  38.1 0.0 copy-done
  38.1 0.6 %copy.23 = f32[3,1,1,1,32]{4,3,2,1,0:T(1,128)} copy(f32[3,1,1,1,32]{4,3,2,1,0:T(1,128)S(1)} %copy-done) | data formatting | bytes 768
Async XLA Ops:
  37.0 0.6 %copy-start.1 = (f32[1,1,1,32]{3,2,1,0:T(1,128)S(1)}, f32[1,1,1,32]{3,2,1,0:T(1,128)}, u32[]{:S(2)}) copy-start(f32[1,1,1,32]{3,2,1,0:T(1,128)} %get-tuple-element.4) | copy-start | bytes 388
  37.0 1.1 %copy-start = (f32[3,1,1,1,32]{4,3,2,1,0:T(1,128)S(1)}, f32[3,1,1,1,32]{4,3,2,1,0:T(1,128)}, u32[]{:S(2)}) copy-start(f32[3,1,1,1,32]{4,3,2,1,0:T(1,128)} %get-tuple-element.5) | copy-start | bytes 1156

commit v2 on v1

--- a/solution.py
+++ b/solution.py
@@ -30,7 +30,9 @@
 def dg3(a, b, ca, cb):
     ah, al = split(a)
     bh, bl = split(b)
-    return dg(ah, bh, ca, cb) + (dg(ah, bl, ca, cb) + dg(al, bh, ca, cb))
+    left = jnp.concatenate([ah, ah, al], axis=ca)
+    right = jnp.concatenate([bh, bl, bh], axis=cb)
+    return dg(left, right, ca, cb)
 
 
 def parts(x):
@@ -54,16 +56,14 @@
     *refs,
 ):
     hbm = refs[:INPUTS]
-    energy_ref, force_ref = refs[INPUTS : INPUTS + 2]
-    held = refs[INPUTS + 2 : 2 * INPUTS + 2]
-    body(sizes, hbm, energy_ref, force_ref, held, *refs[2 * INPUTS + 2 :])
+    held = refs[INPUTS + 1 : 2 * INPUTS + 1]
+    body(sizes, hbm, refs[INPUTS], held, *refs[2 * INPUTS + 1 :])
 
 
 def body(
     sizes,
     hbm,
-    energy_ref,
-    force_ref,
+    out_ref,
     held,
     own8,
     gpos_in,
@@ -271,33 +271,27 @@
         weight = harm[m] * env * (1.0 / mean_degree)
         pool[atoms * m : atoms * (m + 1), :] = jnp.where(near, weight, 0.0).astype(BF16)
 
-    centres = lax.broadcasted_iota(jnp.int32, (nb, edges), 0).astype(F32) / (nb - 1)
-
-    def basis_of():
-        return jnp.exp(-jnp.square((rows[3:4] - centres) * nb))
+    centres = lax.broadcasted_iota(jnp.int32, (nb, CH), 0).astype(F32) / (nb - 1)
+
+    def gap_of(e):
+        return rows[3:4, e : e + CH] - centres
 
     def radial(t):
-        basis = basis_of()
-        bh = basis.astype(BF16).astype(F32)
-        bl = basis - bh
         wi = win_ref[t]
         wh = wi.astype(BF16).astype(F32)
         wl = wi - wh
-        pre = dg(
-            jnp.concatenate([wh, wh, wl, wl], axis=0).astype(BF16),
-            jnp.concatenate([bh, bl, bh, bl], axis=0).astype(BF16),
-            0,
-            0,
-        )
-        pre_s[t] = pre
-        hidden = pre * jax.nn.sigmoid(pre)
-        hh, hl = split(hidden)
+        wi = jnp.concatenate([wh, wh, wl, wl], axis=0).T.astype(BF16)
         wo = wout_ref[t]
         oh = wo.astype(BF16).astype(F32)
         left = jnp.concatenate([oh, oh, wo - oh], axis=0).T.astype(BF16)
-        right = jnp.concatenate([hh, hl, hh], axis=0)
         for e in range(0, edges, CH):
-            rad[t, :, e : e + CH] = dg(left, right[:, e : e + CH], 1, 0)
+            basis = jnp.exp(-jnp.square(gap_of(e) * nb))
+            bh = basis.astype(BF16).astype(F32)
+            bl = basis - bh
+            pre = dg(wi, jnp.concatenate([bh, bl, bh, bl], axis=0).astype(BF16), 1, 0)
+            pre_s[t, :, e : e + CH] = pre
+            hh, hl = split(pre * jax.nn.sigmoid(pre))
+            rad[t, :, e : e + CH] = dg(left, jnp.concatenate([hh, hl, hh], axis=0), 1, 0)
 
     def pooled(t):
         for e in range(0, edges, CH):
@@ -341,6 +335,10 @@
 
     def edge_rows(t, d_a):
         span = [(0, 1), (1, 4), (4, 9)]
+        wo = jnp.concatenate(split(wout_ref[t]), axis=0)
+        wi = win_ref[t]
+        wh = wi.astype(BF16).astype(F32)
+        wi = jnp.concatenate([wh, wh, wi - wh], axis=1).astype(BF16)
         for e in range(0, edges, CH):
             pick = ohr[:, e : e + CH].astype(F32)
             for k, (lo, hi) in enumerate(span):
@@ -352,18 +350,19 @@
                         drow[m : m + 1, e : e + CH] = line
                     else:
                         drow[m : m + 1, e : e + CH] += line
-        d_hidden = dg(jnp.concatenate(split(wout_ref[t]), axis=0), der[...], 1, 0)
-        d_hidden = d_hidden[0:rh] + d_hidden[rh : 2 * rh]
-        pre = pre_s[t]
-        sig = jax.nn.sigmoid(pre)
-        d_pre = d_hidden * (sig * (1.0 + pre * (1.0 - sig)))
-        d_basis = dg3(win_ref[t], d_pre, 1, 0)
-        gap = rows[3:4] - centres
-        slope = jnp.sum(d_basis * basis_of() * gap, axis=0, keepdims=True) * (-2.0 * nb * nb)
-        if t == 1:
-            drow[9:10] = slope
-        else:
-            drow[9:10] += slope
+            d_hidden = dg(wo, der[:, e : e + CH], 1, 0)
+            d_hidden = d_hidden[0:rh] + d_hidden[rh : 2 * rh]
+            pre = pre_s[t, :, e : e + CH]
+            sig = jax.nn.sigmoid(pre)
+            ph, pl_ = split(d_hidden * (sig * (1.0 + pre * (1.0 - sig))))
+            d_basis = dg(wi, jnp.concatenate([ph, pl_, ph], axis=0), 1, 0)
+            gap = gap_of(e)
+            d_basis = d_basis * jnp.exp(-jnp.square(gap * nb)) * gap
+            slope = jnp.sum(d_basis, axis=0, keepdims=True) * (-2.0 * nb * nb)
+            if t == 1:
+                drow[9:10, e : e + CH] = slope
+            else:
+                drow[9:10, e : e + CH] += slope
 
     radial(0)
     prod1, a1_one, a2_one = pooled(0)
@@ -391,7 +390,8 @@
     rout = jnp.sum(jnp.where(eye, rout_ref[...], 0.0), axis=1, keepdims=True)
     ro_sig = jax.nn.sigmoid(ro_pre)
     energy2 = jnp.sum(ro_pre * ro_sig * rout, axis=0, keepdims=True)
-    energy_ref[0, 0] = (energy1 + energy2) * atom_row
+    out_ref[...] = jnp.zeros_like(out_ref)
+    out_ref[3:4, 0:atoms] = (energy1 + energy2) * atom_row
 
     d_ro = rout * atom_row * (ro_sig * (1.0 + ro_pre * (1.0 - ro_sig)))
     d_h2 = dg3(d_ro, rhid_ref[...], 0, 0)
@@ -436,7 +436,7 @@
     both = jnp.concatenate([d_hi, d_rel - d_hi], axis=0).astype(BF16)
     fourth = []
     for t in range(tiles):
-        back = dg(both, ohs[t * 128 : (t + 1) * 128], 1, 1)
+        back = dg(ohs[t * 128 : (t + 1) * 128], both, 1, 1).T
         dp_out[t] = back[0:8] + back[8:16]
         fourth += exchange(3, lambda u: dp_out.at[u // 4], dp_in, 1, t)
     dp_in[here] = dp_out[here // 4]
@@ -451,8 +451,7 @@
     fold = fold + pltpu.roll(fold, 64, 1)
     fold = fold + pltpu.roll(fold, 32, 1)
     force = own[0:8] + own[8:16] - fold[:, 0:atoms]
-    for a in range(3):
-        force_ref[a, 0, 0] = force[a : a + 1]
+    out_ref[0:3, 0:atoms] = force[0:3]
     for c in sent:
         c.wait_send()
 
@@ -502,14 +501,11 @@
         read_out.reshape(1, -1),
     )
     vmem = pl.BlockSpec(memory_space=pltpu.VMEM)
-    energy, force = pl.pallas_call(
+    out = pl.pallas_call(
         functools.partial(kernel, sizes),
-        out_shape=(
-            jax.ShapeDtypeStruct((1, 1, 1, atoms), F32),
-            jax.ShapeDtypeStruct((3, 1, 1, 1, atoms), F32),
-        ),
+        out_shape=jax.ShapeDtypeStruct((8, 128), F32),
         in_specs=[pl.BlockSpec(memory_space=pltpu.HBM)] * INPUTS,
-        out_specs=(vmem, vmem),
+        out_specs=vmem,
         scratch_shapes=[pltpu.VMEM(a.shape, a.dtype) for a in operands]
         + [
             pltpu.VMEM((8, 128), F32),
@@ -540,7 +536,8 @@
             collective_id=0, has_side_effects=True, vmem_limit_bytes=64 * 1024 * 1024
         ),
     )(*operands)
-    return energy, force
+    energy = out[3, 0:atoms].reshape(1, 1, 1, atoms)
+    return energy, out[0:3, 0:atoms].reshape(3, 1, 1, 1, atoms)
 
 
 def solution(mesh):

time: 38.9 us -> 40.9 us (1.051)
  Pallas kernels: 35 us -> 36.3 us
  local copies, waits for them, and re-layouts: 1.69 us -> 2.44 us
    pallas_call x1, Pallas kernels: 35 us -> 36.3 us  [local(): pl.pallas_call(functools.partial(kernel, sizes), out_shape=jax.ShapeDtype...]
    another operation x0 -> x1, local copies, waits for them, and re-layouts: none -> 1.2 us  [local(): energy = out[3, 0:atoms].reshape(1, 1, 1, atoms)]
    unnamed x6 -> x1, local copies, waits for them, and re-layouts: 1.69 us -> 0.57 us
    reshape x0 -> x1, local copies, waits for them, and re-layouts: none -> 0.68 us  [local(): return (energy, out[0:3, 0:atoms].reshape(3, 1, 1, 1, atoms))]
where the time goes in v2:
time: 40.9 us; the launch traced here: 40.7 us
  Pallas kernels  36.3 us (89%)
  local copies, waits for them, and re-layouts  2.44 us (6%)
  between operations  1.94 us (5%)
    pallas_call x1, Pallas kernels, local(): pl.pallas_call(functools.partial(kernel, sizes), out_shape=jax.ShapeDtype...  36.3 us
    another operation x1, local copies, waits for them, and re-layouts, local(): energy = out[3, 0:atoms].reshape(1, 1, 1, atoms)  1.2 us

profile of v2, /device:TPU:0, one launch (start us, length us, event | category | flops | bytes accessed | tf_op | source)
XLA Modules:
  0.0 40.7 jit_solution(17871517591870360922)
XLA Ops:
  1.9 36.3 %shard_map.167 = f32[8,128]{1,0:T(8,128)} custom-call(f32[3,1,1,1,32]{4,3,2,1,0:T(1,128)} %refs_0_.1, s32[1,1,1,32]{3,2,1,0:T(1,128)} %refs_1_.1, s32[1,1,1]{2,1,0:T(1,128)S(6)} %copy.19.refs_2_, s32[1,1,1]{2,1,0:T(1,128)S(6)} %copy.20.refs_3_, s32[1,1,1,1792]{3,2,1,0:T(1,128)} %refs_4_.1, s32[1,1,1,1792]{3,2,1,0:T(1,128)} %refs_5_.1, ...), custom_call_target="tpu_custom_call" | custom-call | tf_op jit(solution)/shard_map/pallas_call | solution.py:504
  38.2 1.2 %slice_bitcast_fusion.1 = f32[1,1,1,32]{3,2,1,0:T(1,128)} fusion(f32[8,128]{1,0:T(8,128)} %shard_map.167), kind=kLoop, calls=%fused_computation.1 | loop fusion | bytes 256 | tf_op jit(solution)/shard_map/reshape;squeeze | solution.py:539
  39.4 0.7 %slice_bitcast_fusion = f32[3,1,1,1,32]{4,0,3,2,1:T(4,128)S(1)} fusion(f32[8,128]{1,0:T(8,128)} %shard_map.167), kind=kLoop, calls=%fused_computation | loop fusion | bytes 768 | tf_op jit(solution)/shard_map/reshape | solution.py:540
  40.1 0.6 %copy.18 = f32[3,1,1,1,32]{4,3,2,1,0:T(1,128)} copy(f32[3,1,1,1,32]{4,0,3,2,1:T(4,128)S(1)} %slice_bitcast_fusion) | data formatting | bytes 768

commit v3 on v1

--- a/solution.py
+++ b/solution.py
@@ -111,8 +111,6 @@
         pltpu.make_async_copy(src, dst, in_sem.at[i])
         for i, (src, dst) in enumerate(zip(hbm, held))
     ]
-    for c in fetch:
-        c.start()
     atoms = pos_ref.shape[-1]
     edges = sender_ref.shape[-1]
     nb = win_ref.shape[1]
@@ -137,6 +135,8 @@
     barrier = pltpu.get_barrier_semaphore()
     for u in others:
         pl.semaphore_signal(barrier, inc=1, device_id=device(offs[u], 1), device_id_type=MESH)
+    for c in fetch:
+        c.start()
 
     own8[...] = jnp.zeros_like(own8)
     fetch[0].wait()
@@ -157,8 +157,6 @@
             device_id_type=MESH,
         )
 
-    sent = []
-
     def exchange(phase, source, target, sign, tile=None):
         started = [
             copy(phase, u, source(u), target.at[u], sign)
@@ -167,7 +165,6 @@
         ]
         for c in started:
             c.start()
-        sent.extend(started)
         return started
 
     first = exchange(0, lambda u: own8, gpos_in, -1)
@@ -374,6 +371,14 @@
     rone = jnp.broadcast_to(rone_ref[...], (8, width))
     energy1 = dg3(rone, h1, 1, 1)[0:1]
     radial(1)
+    rhid = rhid_ref[...]
+    mixed = dg3(rhid, wmix_ref[1], 1, 1)
+    lifted_mix = dg3(wmix_ref[0], wup_ref[1], 1, 0)
+    ro_own = dg3(rhid, h_own[...].astype(F32), 1, 1)
+    eye = lax.broadcasted_iota(jnp.int32, (rhid.shape[0],) * 2, 0) == (
+        lax.broadcasted_iota(jnp.int32, (rhid.shape[0],) * 2, 1)
+    )
+    rout = jnp.sum(jnp.where(eye, rout_ref[...], 0.0), axis=1, keepdims=True)
     wt_h, wt_l = split(wup_ref[1].T)
     for c in second:
         c.wait_recv()
@@ -383,19 +388,13 @@
     for e in range(0, edges, CH):
         lift[1, :, e : e + CH] = dg(ghost_lift, ohs[:, e : e + CH], 1, 0)
     prod2, a1_two, a2_two = pooled(1)
-    h2 = h_own[...].astype(F32) + dg3(prod2, wmix_ref[1], 1, 0)
-    ro_pre = dg3(rhid_ref[...], h2, 1, 1)
-    eye = lax.broadcasted_iota(jnp.int32, (ro_pre.shape[0],) * 2, 0) == (
-        lax.broadcasted_iota(jnp.int32, (ro_pre.shape[0],) * 2, 1)
-    )
-    rout = jnp.sum(jnp.where(eye, rout_ref[...], 0.0), axis=1, keepdims=True)
+    ro_pre = ro_own + dg3(mixed, prod2, 1, 1)
     ro_sig = jax.nn.sigmoid(ro_pre)
     energy2 = jnp.sum(ro_pre * ro_sig * rout, axis=0, keepdims=True)
     energy_ref[0, 0] = (energy1 + energy2) * atom_row
 
     d_ro = rout * atom_row * (ro_sig * (1.0 + ro_pre * (1.0 - ro_sig)))
-    d_h2 = dg3(d_ro, rhid_ref[...], 0, 0)
-    d_prod2 = dg3(d_h2, wmix_ref[1], 1, 1)
+    d_prod2 = dg3(d_ro, mixed, 0, 0)
     d_a = pulled(1, d_prod2, a1_two, a2_two)
     third = []
     for t in range(tiles):
@@ -406,14 +405,15 @@
         third += exchange(2, lambda u: dl_out.at[u], dl_in, 1, t)
     dl_in[here] = dl_out[here]
     edge_rows(1, d_a)
+    d_own1 = dg3(d_ro, rhid, 0, 0) + atom_col * rone_ref[...]
+    d_prod1 = dg3(d_own1, wmix_ref[0], 1, 1)
     for c in third:
         c.wait_recv()
 
     gathered = dl_in[0].astype(F32)
     for u in range(1, total):
         gathered = gathered + dl_in[u].astype(F32)
-    d_h1 = d_h2 + dg3(gathered, wup_ref[1], 1, 1) + atom_col * rone_ref[...]
-    d_prod1 = dg3(d_h1, wmix_ref[0], 1, 1)
+    d_prod1 = d_prod1 + dg3(gathered, lifted_mix, 1, 1)
     d_a = pulled(0, d_prod1, a1_one, a2_one)
     edge_rows(0, d_a)
 
@@ -441,6 +441,8 @@
         fourth += exchange(3, lambda u: dp_out.at[u // 4], dp_in, 1, t)
     dp_in[here] = dp_out[here // 4]
     own = dg(both, ohr[...], 1, 1)
+    for c in first + second + third:
+        c.wait_send()
     for c in fourth:
         c.wait_recv()
     fold = jnp.zeros((8, 128), F32)
@@ -453,7 +455,7 @@
     force = own[0:8] + own[8:16] - fold[:, 0:atoms]
     for a in range(3):
         force_ref[a, 0, 0] = force[a : a + 1]
-    for c in sent:
+    for c in fourth:
         c.wait_send()
 
 

time: 38.9 us -> 38.2 us (0.982)
  Pallas kernels: 35 us -> 34.3 us
    pallas_call x1, Pallas kernels: 35 us -> 34.3 us  [local(): pl.pallas_call(functools.partial(kernel, sizes), out_shape=(jax.ShapeDtyp...]
where the time goes in v3:
time: 38.2 us; the launch traced here: 38 us
  Pallas kernels  34.3 us (90%)
  between operations  1.95 us (5%)
  local copies, waits for them, and re-layouts  1.69 us (4%)
    pallas_call x1, Pallas kernels, local(): pl.pallas_call(functools.partial(kernel, sizes), out_shape=(jax.ShapeDtyp...  34.3 us
    unnamed x6, local copies, waits for them, and re-layouts  1.69 us

profile of v3, /device:TPU:0, one launch (start us, length us, event | category | flops | bytes accessed | tf_op | source)
XLA Modules:
  0.0 38.0 jit_solution(1607264488008403085)
XLA Ops:
  1.9 34.3 %shard_map.167 = (f32[1,1,1,32]{3,2,1,0:T(1,128)}, f32[3,1,1,1,32]{4,3,2,1,0:T(1,128)}) custom-call(f32[3,1,1,1,32]{4,3,2,1,0:T(1,128)} %refs_0_.1, s32[1,1,1,32]{3,2,1,0:T(1,128)} %refs_1_.1, s32[1,1,1]{2,1,0:T(1,128)S(6)} %copy.20.refs_2_, s32[1,1,1]{2,1,0:T(1,128)S(6)} %copy.21.refs_3_, s32[1,1,1,1792]{3,2,1,0:T(1,128)} %refs_4_.1, ...), custom_call_target="tpu_custom_call" | custom-call | tf_op jit(solution)/shard_map/pallas_call | solution.py:507
  36.3 0.0 copy-start.1
  36.3 0.0 copy-start
  36.3 0.6 %copy-done.1 = f32[1,1,1,32]{3,2,1,0:T(1,128)S(1)} copy-done((f32[1,1,1,32]{3,2,1,0:T(1,128)S(1)}, f32[1,1,1,32]{3,2,1,0:T(1,128)}, u32[]{:S(2)}) %copy-start.1) | copy-done | bytes 152
  36.9 0.5 %copy.22 = f32[1,1,1,32]{3,2,1,0:T(1,128)} copy(f32[1,1,1,32]{3,2,1,0:T(1,128)S(1)} %copy-done.1) | data formatting | bytes 256
  37.4 0.0 copy-done
  37.4 0.6 %copy.23 = f32[3,1,1,1,32]{4,3,2,1,0:T(1,128)} copy(f32[3,1,1,1,32]{4,3,2,1,0:T(1,128)S(1)} %copy-done) | data formatting | bytes 768
Async XLA Ops:
  36.3 0.6 %copy-start.1 = (f32[1,1,1,32]{3,2,1,0:T(1,128)S(1)}, f32[1,1,1,32]{3,2,1,0:T(1,128)}, u32[]{:S(2)}) copy-start(f32[1,1,1,32]{3,2,1,0:T(1,128)} %get-tuple-element.4) | copy-start | bytes 388
  36.3 1.1 %copy-start = (f32[3,1,1,1,32]{4,3,2,1,0:T(1,128)S(1)}, f32[3,1,1,1,32]{4,3,2,1,0:T(1,128)}, u32[]{:S(2)}) copy-start(f32[3,1,1,1,32]{4,3,2,1,0:T(1,128)} %get-tuple-element.5) | copy-start | bytes 1156

commit v4 on v3

--- a/solution.py
+++ b/solution.py
@@ -131,6 +131,7 @@
         )
 
     others = [u for u in range(total) if u != here]
+    others.sort(key=lambda u: -sum(o != 0 for o in offs[u]))
 
     barrier = pltpu.get_barrier_semaphore()
     for u in others:
@@ -324,17 +325,26 @@
         ]
         d_t = [d.T.astype(BF16) for d in d_a]
         d_a = [d.astype(BF16) for d in d_a]
-        span = [(0, 1), (1, 4), (4, 9)]
+        for e in range(0, edges, CH):
+            if t == 1:
+                d_up = jnp.zeros((width, CH), F32)
+                for k in range(3):
+                    piece = rad[t, k * width : (k + 1) * width, e : e + CH]
+                    d_up = d_up + d_base_of(d_t, k, e) * piece
+                dlift[:, e : e + CH] = d_up.astype(BF16)
+        return d_a, d_t
+
+    def d_base_of(d_t, k, e):
+        lo, hi = ((0, 1), (1, 4), (4, 9))[k]
+        return dg(d_t[k], pool[lo * atoms : hi * atoms, e : e + CH], 1, 0)
+
+    def radial_pulled(t, d_t):
         for e in range(0, edges, CH):
             up = lift[t, :, e : e + CH]
-            d_up = jnp.zeros((width, CH), F32)
-            for k, (lo, hi) in enumerate(span):
-                d_base = dg(d_t[k], pool[lo * atoms : hi * atoms, e : e + CH], 1, 0)
-                d_up = d_up + d_base * rad[t, k * width : (k + 1) * width, e : e + CH]
-                der[k * width : (k + 1) * width, e : e + CH] = (d_base * up).astype(BF16)
-            if t == 1:
-                dlift[:, e : e + CH] = d_up.astype(BF16)
-        return d_a
+            for k in range(3):
+                der[k * width : (k + 1) * width, e : e + CH] = (
+                    d_base_of(d_t, k, e) * up
+                ).astype(BF16)
 
     def edge_rows(t, d_a):
         span = [(0, 1), (1, 4), (4, 9)]
@@ -395,7 +405,7 @@
 
     d_ro = rout * atom_row * (ro_sig * (1.0 + ro_pre * (1.0 - ro_sig)))
     d_prod2 = dg3(d_ro, mixed, 0, 0)
-    d_a = pulled(1, d_prod2, a1_two, a2_two)
+    d_a, d_t = pulled(1, d_prod2, a1_two, a2_two)
     third = []
     for t in range(tiles):
         d_ghost = dg(ohs[t * 128 : (t + 1) * 128], dlift[...], 1, 1)
@@ -404,6 +414,7 @@
                 dl_out[4 * t + j] = d_ghost[32 * j : 32 * j + 32].astype(BF16)
         third += exchange(2, lambda u: dl_out.at[u], dl_in, 1, t)
     dl_in[here] = dl_out[here]
+    radial_pulled(1, d_t)
     edge_rows(1, d_a)
     d_own1 = dg3(d_ro, rhid, 0, 0) + atom_col * rone_ref[...]
     d_prod1 = dg3(d_own1, wmix_ref[0], 1, 1)
@@ -414,7 +425,8 @@
     for u in range(1, total):
         gathered = gathered + dl_in[u].astype(F32)
     d_prod1 = d_prod1 + dg3(gathered, lifted_mix, 1, 1)
-    d_a = pulled(0, d_prod1, a1_one, a2_one)
+    d_a, d_t = pulled(0, d_prod1, a1_one, a2_one)
+    radial_pulled(0, d_t)
     edge_rows(0, d_a)
 
     x, y, z, inner = rows[0:1], rows[1:2], rows[2:3], rows[4:5]

time: 38.2 us -> 37.4 us (0.979)
  Pallas kernels: 34.3 us -> 33.6 us
    pallas_call x1, Pallas kernels: 34.3 us -> 33.6 us  [local(): pl.pallas_call(functools.partial(kernel, sizes), out_shape=(jax.ShapeDtyp...]
where the time goes in v4:
time: 37.4 us; the launch traced here: 37.2 us
  Pallas kernels  33.6 us (90%)
  between operations  1.95 us (5%)
  local copies, waits for them, and re-layouts  1.69 us (5%)
    pallas_call x1, Pallas kernels, local(): pl.pallas_call(functools.partial(kernel, sizes), out_shape=(jax.ShapeDtyp...  33.6 us
    unnamed x6, local copies, waits for them, and re-layouts  1.69 us

profile of v4, /device:TPU:0, one launch (start us, length us, event | category | flops | bytes accessed | tf_op | source)
XLA Modules:
  0.0 37.2 jit_solution(4478053473230896135)
XLA Ops:
  1.9 33.6 %shard_map.167 = (f32[1,1,1,32]{3,2,1,0:T(1,128)}, f32[3,1,1,1,32]{4,3,2,1,0:T(1,128)}) custom-call(f32[3,1,1,1,32]{4,3,2,1,0:T(1,128)} %refs_0_.1, s32[1,1,1,32]{3,2,1,0:T(1,128)} %refs_1_.1, s32[1,1,1]{2,1,0:T(1,128)S(6)} %copy.20.refs_2_, s32[1,1,1]{2,1,0:T(1,128)S(6)} %copy.21.refs_3_, s32[1,1,1,1792]{3,2,1,0:T(1,128)} %refs_4_.1, ...), custom_call_target="tpu_custom_call" | custom-call | tf_op jit(solution)/shard_map/pallas_call | solution.py:519
  35.5 0.0 copy-start.1
  35.5 0.0 copy-start
  35.5 0.6 %copy-done.1 = f32[1,1,1,32]{3,2,1,0:T(1,128)S(1)} copy-done((f32[1,1,1,32]{3,2,1,0:T(1,128)S(1)}, f32[1,1,1,32]{3,2,1,0:T(1,128)}, u32[]{:S(2)}) %copy-start.1) | copy-done | bytes 152
  36.1 0.5 %copy.22 = f32[1,1,1,32]{3,2,1,0:T(1,128)} copy(f32[1,1,1,32]{3,2,1,0:T(1,128)S(1)} %copy-done.1) | data formatting | bytes 256
  36.6 0.0 copy-done
  36.6 0.6 %copy.23 = f32[3,1,1,1,32]{4,3,2,1,0:T(1,128)} copy(f32[3,1,1,1,32]{4,3,2,1,0:T(1,128)S(1)} %copy-done) | data formatting | bytes 768
Async XLA Ops:
  35.5 0.6 %copy-start.1 = (f32[1,1,1,32]{3,2,1,0:T(1,128)S(1)}, f32[1,1,1,32]{3,2,1,0:T(1,128)}, u32[]{:S(2)}) copy-start(f32[1,1,1,32]{3,2,1,0:T(1,128)} %get-tuple-element.4) | copy-start | bytes 388
  35.5 1.1 %copy-start = (f32[3,1,1,1,32]{4,3,2,1,0:T(1,128)S(1)}, f32[3,1,1,1,32]{4,3,2,1,0:T(1,128)}, u32[]{:S(2)}) copy-start(f32[3,1,1,1,32]{4,3,2,1,0:T(1,128)} %get-tuple-element.5) | copy-start | bytes 1156
